TPU v7x, 32 devices: a whole 2x2x4 slice. The times are simulated.
32 devices in a mesh: dp: 4 (over y, x), space: 8 (over z, core).
Axes of the slice: x: 2, y: 2, z: 4, core: 2. Of those that a mesh axis runs over, the one named last changes fastest.
Arguments:
- features: bfloat16 [4, 128, 128, 256], P('dp', 'space'), may hold values from -6 to 6
- heights: float32 [4, 128, 128], P('dp', 'space'), may hold values from 0.02 to 2
- cotangent: bfloat16 [4, 128, 128, 256], P('dp', 'space'), may hold values from -6 to 6
- weight_first: bfloat16 [3, 3, 256, 256], replicated, may hold values from -0.125 to 0.125
- weight_second: bfloat16 [3, 3, 256, 256], replicated, may hold values from -0.125 to 0.125
- shade_embed: bfloat16 [256], replicated, may hold values from -4 to 4
Outputs:
- grad_features: bfloat16 [4, 128, 128, 256], P('dp', 'space')
- grad_first: float32 [3, 3, 256, 256], replicated
- grad_second: float32 [3, 3, 256, 256], replicated
- grad_embed: float32 [256], replicated
All inputs are finite; a program needn't handle non-finite values.
Results may differ from a plain program's by a relative error of at most 0.012.
Values may be sent and summed in bfloat16 or wider, within the bound.
A program may use at most 64 MiB of HBM per device.

v0:
```python
import math

import jax
import jax.numpy as jnp
from jax import lax
from jax.sharding import PartitionSpec as P


def prefix(part, axis, combine, identity):
    place = lax.axis_index(axis)
    gathered = lax.all_gather(part, axis)
    state = jnp.zeros_like(part) + jnp.asarray(identity, part.dtype)

    def one(hop, state):
        return combine(state, lax.dynamic_index_in_dim(gathered, hop, 0, False))

    return lax.fori_loop(0, place, one, state)


def padded_2(cells, sides, width):
    for axis, dim in sides:
        count = lax.axis_size(axis)
        ends = count - 1
        head = lax.slice_in_dim(cells, 0, width, axis=dim)
        tail = lax.slice_in_dim(cells, cells.shape[dim] - width, cells.shape[dim], axis=dim)
        cells = jnp.concatenate(
            [
                lax.ppermute(tail, axis, [(i, (i + 1) % count) for i in range(ends)]),
                cells,
                lax.ppermute(head, axis, [((i + 1) % count, i) for i in range(ends)]),
            ],
            axis=dim,
        )
    return cells


def convolve(padded, kernel):
    return lax.conv_general_dilated(
        padded,
        kernel,
        (1, 1),
        ((0, 0), (1, 1)),
        dimension_numbers=("NHWC", "HWIO", "NHWC"),
        preferred_element_type=jnp.float32,
    )


def reversed_kernel(kernel):
    return jnp.transpose(jnp.flip(kernel, (0, 1)), (0, 1, 3, 2))


def silu_slope(values):
    sigma = jax.nn.sigmoid(values)
    return sigma * (1.0 + values * (1.0 - sigma))


def kernel_grad(padded, gradient):
    channels = gradient.shape[-1]
    row_count = gradient.shape[1]
    col_count = gradient.shape[2]
    widened = jnp.pad(padded, ((0, 0), (0, 0), (1, 1), (0, 0)))
    flat_grad = gradient.reshape(-1, channels)
    stacked = []
    for offset_row in range(3):
        line = []
        for offset_col in range(3):
            window = widened[
                :, offset_row : offset_row + row_count, offset_col : offset_col + col_count, :
            ].reshape(-1, channels)
            line.append(jnp.dot(window.T, flat_grad, preferred_element_type=jnp.float32))
        stacked.append(jnp.stack(line))
    return jnp.stack(stacked)


def body(features, heights, cotangent, weight_first, weight_second, shade_embed):
    images, strip, col_count, channels = features.shape
    space_count = lax.axis_size("space")
    total_rows = strip * space_count
    decline = 2.0 / total_rows
    strip_index = lax.axis_index("space")
    position = (strip_index * strip + jnp.arange(strip)).astype(jnp.float32)
    lifted = heights + decline * position[None, :, None]
    strip_peak = jnp.max(lifted, axis=1)
    carried = prefix(strip_peak, "space", jnp.maximum, jnp.zeros_like(strip_peak))
    running = lax.cummax(lifted, axis=1)
    earlier_max = jnp.concatenate(
        [carried[:, None, :], jnp.maximum(running[:, :-1, :], carried[:, None, :])], axis=1
    )
    shading = jnp.maximum(earlier_max - lifted, 0.0)
    mixed = (
        features.astype(jnp.float32) + shading[..., None] * shade_embed.astype(jnp.float32)
    ).astype(jnp.bfloat16)
    back_second = reversed_kernel(weight_second)
    back_first = reversed_kernel(weight_first)
    padded_in = padded_2(mixed, (("space", 1),), 1)
    hidden_pre = convolve(padded_in, weight_first)
    active = jax.nn.silu(hidden_pre).astype(jnp.bfloat16)
    active_pad = padded_2(active, (("space", 1),), 1)
    cot_pad = padded_2(cotangent, (("space", 1),), 1)
    back_act = convolve(cot_pad, back_second)
    back_hidden = (back_act * silu_slope(hidden_pre)).astype(jnp.bfloat16)
    hidden_pad = padded_2(back_hidden, (("space", 1),), 1)
    back_input = convolve(hidden_pad, back_first)
    grad_features = (cotangent.astype(jnp.float32) + back_input).astype(jnp.bfloat16)
    scaling = 1.0 / math.sqrt(images * lax.axis_size("dp") * total_rows * col_count)
    first_term = kernel_grad(padded_in, back_hidden).reshape(-1) * scaling
    second_term = kernel_grad(active_pad, cotangent).reshape(-1) * scaling
    embed_term = jnp.sum(shading[..., None] * back_input, axis=(0, 1, 2)) * scaling
    first_sum, second_sum, embed_sum = lax.psum(
        (first_term, second_term, embed_term), ("dp", "space")
    )
    kernel_shape = (3, 3, channels, channels)
    return (
        grad_features,
        first_sum.reshape(kernel_shape),
        second_sum.reshape(kernel_shape),
        embed_sum,
    )


def solution(mesh):
    in_specs = (
        P("dp", "space", None, None),
        P("dp", "space", None),
        P("dp", "space", None, None),
        P(),
        P(),
        P(),
    )
    out_specs = (P("dp", "space", None, None), P(), P(), P())
    return jax.shard_map(body, mesh=mesh, in_specs=in_specs, out_specs=out_specs, check_vma=False)
```

profile of v0, /device:TPU:0, one launch (start us, length us, event | category | flops | bytes accessed | tf_op | source)
XLA Modules:
  0.0 250.0 jit_solution(15768503703791382896)
XLA Ops:
  8.8 13.4 %all-gather.1 = f32[8,1,128]{2,1,0:T(1,128)S(1)} all-gather(f32[1,1,128]{2,1,0:T(1,128)S(1)} %bitcast.222), channel_id=2, replica_groups=mesh['dp'=4,'space'=8] {'space'}, dimensions={0}, use_global_device_ids=true | all-gather | bytes 4608 | tf_op jit(solution)/shard_map/all_gather | solution.py:11
  22.1 1.7 copy.38
  24.3 2.2 collective-permute-start.2
  26.6 1.3 collective-permute-start.3
  28.5 3.6 %collective-permute-start = (bf16[1,1,128,256]{3,2,1,0:T(8,128)(2,1)}, bf16[1,1,128,256]{3,2,1,0:T(8,128)(2,1)}, u32[]{:S(2)}, u32[]{:S(2)}) collective-permute-start(bf16[1,1,128,256]{3,2,1,0:T(8,128)(2,1)} %get-tuple-element.60), channel_id=1, source_target_pairs={{0,1},{1,2},{2,3},{3,4},{4,5},{5,6},{6,7},{8,9},{9,10},{10,11},{11... | collective-permute-start | bytes 196616 | tf_op jit(solution)/shard_map/ppermute | solution.py:28
  32.2 1.3 collective-permute-start.1
  33.5 1.2 pad_maximum_fusion
  34.7 1.4 copy.62
  36.1 1.7 pad.11.clone
  37.9 1.4 reshape.171
  39.3 1.8 copy.41
  41.2 4.4 %multiply_convert_fusion.1 = (bf16[16,8,17,256]{3,1,2,0:T(8,128)(2,1)S(1)}, f32[16,8,17,256]{3,1,2,0:T(8,128)}) fusion(pred[8,17]{0,1:T(8,128)(4,1)S(1)} %copy-done.27, bf16[3,3,256,256]{3,2,1,0:T(8,128)(2,1)S(1)} %copy-done, bf16[18,1,7,2,256]{4,2,3,0,1:T(8,128)(2,1)S(1)} %slice.130, bf16[18,1,8,17,256]{4,2,3,0,1:T(8,128)(2,1)S(1)} %copy.41), kind=kOutput, calls=%fused_computation.22 | convolution fusion | flops 2574458880 | bytes 5904520 | tf_op jit(solution)/shard_map/conv_general_dilated | solution.py:38
  46.2 1.2 copy.52
  47.4 1.0 maximum_bitcast_fusion
  49.0 1.4 reshape.166
  50.5 1.9 copy.37
  52.4 4.7 %multiply_convert_fusion = bf16[16,8,17,256]{3,1,2,0:T(8,128)(2,1)S(1)} fusion(f32[16,8,17,256]{3,1,2,0:T(8,128)} %get-tuple-element.65, bf16[3,3,256,256]{3,2,1,0:T(8,128)(2,1)S(1)} %copy-done.26, bf16[18,1,7,2,256]{4,2,3,0,1:T(8,128)(2,1)S(1)} %slice.126, bf16[18,1,8,17,256]{4,2,3,0,1:T(8,128)(2,1)S(1)} %copy.37, pred[8,17]{0,1:T(8,128)(4,1)S(1)} %copy-done.27), kind=kOutput, calls=%fused_computation.21 | convolution fusion | flops 2577244160 | bytes 5904520 | tf_op jit(solution)/shard_map/conv_general_dilated | solution.py:38
  57.4 1.3 copy-done.3
  58.8 1.5 convolution_bitcast_fusion.13
  60.3 1.5 convolution_bitcast_fusion.17
  61.8 1.5 convolution_bitcast_fusion.9
  63.3 1.5 convolution_bitcast_fusion.11
  64.9 1.5 convolution_bitcast_fusion.12
  66.4 1.5 convolution_bitcast_fusion.14
  67.9 1.5 convolution_bitcast_fusion.15
  69.5 1.0 slice.140
  70.5 1.9 copy.60
  73.3 3.8 %collective-permute-start.6 = (bf16[1,1,128,256]{2,3,1,0:T(8,128)(2,1)}, bf16[1,1,128,256]{2,3,1,0:T(8,128)(2,1)}, u32[]{:S(2)}, u32[]{:S(2)}) collective-permute-start(bf16[1,1,128,256]{2,3,1,0:T(8,128)(2,1)} %copy.59), channel_id=1, source_target_pairs={{0,1},{1,2},{2,3},{3,4},{4,5},{5,6},{6,7},{8,9},{9,10},{10,11},{11... | collective-permute-start | bytes 196616 | tf_op jit(solution)/shard_map/ppermute | solution.py:28
  77.3 1.4 collective-permute-start.7
  81.6 1.6 maximum_multiply_fusion
  83.2 2.3 fusion.8
  89.0 1.3 convolution_bitcast_fusion.7
  90.4 1.6 maximum_multiply_fusion.1
  93.8 3.7 %collective-permute-start.4 = (bf16[1,1,128,256]{3,2,1,0:T(8,128)(2,1)}, bf16[1,1,128,256]{3,2,1,0:T(8,128)(2,1)S(1)}, u32[]{:S(2)}, u32[]{:S(2)}) collective-permute-start(bf16[1,1,128,256]{3,2,1,0:T(8,128)(2,1)} %slice.132), channel_id=1, source_target_pairs={{0,1},{1,2},{2,3},{3,4},{4,5},{5,6},{6,7},{8,9},{9,10},{10,11},{11... | collective-permute-start | bytes 196616 | tf_op jit(solution)/shard_map/ppermute | solution.py:28
  98.1 1.3 collective-permute-start.5
  99.4 1.4 copy.35
  101.1 1.6 collective-permute-done.5
  102.9 1.7 pad.13
  104.5 2.3 reshape.188
  107.2 3.0 %convolution_select_fusion = f32[16,8,17,256]{3,1,2,0:T(8,128)S(1)} fusion(bf16[3,3,256,256]{3,2,1,0:T(8,128)(2,1)S(1)} %copy-done, bf16[18,1,7,2,256]{4,2,3,0,1:T(8,128)(2,1)S(1)} %slice.136, bf16[18,1,8,17,256]{4,2,3,0,1:T(8,128)(2,1)S(1)} %copy.47, pred[8,17]{0,1:T(8,128)(4,1)S(1)} %copy-done.27), kind=kOutput, calls=%fused_computation.29 | convolution fusion | flops 2571673600 | bytes 4790408 | tf_op jit(solution)/shard_map/conv_general_dilated | solution.py:38
  111.0 1.5 slice.137
  112.5 2.0 copy.58
  114.6 2.7 %fusion.9 = (f32[256]{0:T(256)S(1)}, bf16[1,16,128,256]{2,3,1,0:T(8,128)(2,1)}) fusion(f32[16,1,128,256]{2,3,0,1:T(8,128)S(1)} %copy.58, f32[16,128]{1,0:T(8,128)S(1)} %copy-done.21, bf16[1,16,128,256]{2,3,1,0:T(8,128)(2,1)} %copy.35), kind=kLoop, calls=%fused_computation.26 | loop fusion | flops 2621184 | bytes 4203520 | tf_op jit(solution)/shard_map/reduce_sum | solution.py:108
  117.2 2.3 copy.56
  119.5 42.8 %psum.23 = f32[256]{0:T(256)} all-reduce(f32[256]{0:T(256)S(1)} %broadcast_multiply_fusion), channel_id=1, replica_groups=mesh['dp'=4,'space'=8] {'dp','space'}, use_global_device_ids=true, to_apply=%region_7.8 | all-reduce | flops 256 | bytes 2048 | tf_op jit(solution)/shard_map/psum | solution.py:109
  162.3 76.1 %all-reduce.5.cloned.1.call-done = (f32[3,3,256,256]{3,2,1,0:T(8,128)}, f32[3,3,256,256]{3,2,1,0:T(8,128)}) async-done(((f32[3,3,256,256]{3,2,1,0:T(8,128)}, f32[3,3,256,256]{3,2,1,0:T(8,128)}), (f32[3,3,256,256]{3,2,1,0:T(8,128)}, f32[3,3,256,256]{3,2,1,0:T(8,128)})) %all-reduce.5.cloned.1.call-update) | async-done | bytes 4718608 | tf_op jit(solution)/shard_map/psum | solution.py:109
  238.4 3.4 %copy.109 = f32[3,3,256,256]{3,2,1,0:T(8,128)} copy(f32[3,3,256,256]{3,2,1,0:T(8,128)} %get-tuple-element.118) | data formatting | bytes 4718592
  241.7 1.4 copy.110
  (116 shorter events, 15.5 us)
Async XLA Ops:
  7.2 34.0 %copy-start = (bf16[3,3,256,256]{3,2,1,0:T(8,128)(2,1)S(1)}, bf16[3,3,256,256]{3,2,1,0:T(8,128)(2,1)}, u32[]{:S(2)}) copy-start(bf16[3,3,256,256]{3,2,1,0:T(8,128)(2,1)} %param.11) | copy-start | bytes 3538948
  7.2 231.2 %all-reduce.5.cloned.1.call-start = ((), (), s32[]{:S(2)}) async-start(), calls=%async_computation | async-start | bytes 9437184 | tf_op jit(solution)/shard_map/psum | solution.py:109
  22.1 5.7 %copy-start.1 = (bf16[1,16,128,256]{3,2,1,0:T(8,128)(2,1)S(1)}, bf16[1,16,128,256]{3,2,1,0:T(8,128)(2,1)}, u32[]{:S(2)}) copy-start(bf16[1,16,128,256]{3,2,1,0:T(8,128)(2,1)} %param.10) | copy-start | bytes 3145732
  23.9 9.6 %copy-start.20 = (f32[16,128]{1,0:T(8,128)}, f32[16,128]{1,0:T(8,128)S(1)}, u32[]{:S(2)}) copy-start(f32[16,128]{1,0:T(8,128)S(1)} %fusion.78) | copy-start | bytes 24580
  24.3 9.2 %copy-start.2 = (bf16[1,16,128,256]{2,3,1,0:T(8,128)(2,1)}, bf16[1,16,128,256]{2,3,1,0:T(8,128)(2,1)S(1)}, u32[]{:S(2)}) copy-start(bf16[1,16,128,256]{2,3,1,0:T(8,128)(2,1)S(1)} %add_convert_fusion) | copy-start | bytes 3145732
  24.3 9.1 %collective-permute-start.2 = (bf16[1,1,128,256]{2,3,1,0:T(8,128)(2,1)S(1)}, bf16[1,1,128,256]{2,3,1,0:T(8,128)(2,1)S(1)}, u32[]{:S(2)}, u32[]{:S(2)}) collective-permute-start(bf16[1,1,128,256]{2,3,1,0:T(8,128)(2,1)S(1)} %get-tuple-element.62), channel_id=1, source_target_pairs={{0,1},{1,2},{2,3},{3,4},{4,5},{5,6},{6,7},{8,9},{9,10},{10,11},{11... | collective-permute-start | bytes 196616 | tf_op jit(solution)/shard_map/ppermute | solution.py:28
  26.6 6.9 %collective-permute-start.3 = (bf16[1,1,128,256]{2,3,1,0:T(8,128)(2,1)S(1)}, bf16[1,1,128,256]{2,3,1,0:T(8,128)(2,1)S(1)}, u32[]{:S(2)}, u32[]{:S(2)}) collective-permute-start(bf16[1,1,128,256]{2,3,1,0:T(8,128)(2,1)S(1)} %get-tuple-element.63), channel_id=1, source_target_pairs={{1,0},{2,1},{3,2},{4,3},{5,4},{6,5},{7,6},{9,8},{10,9},{11,10},{12... | collective-permute-start | bytes 196616 | tf_op jit(solution)/shard_map/ppermute | solution.py:30
  28.5 18.9 %collective-permute-start = (bf16[1,1,128,256]{3,2,1,0:T(8,128)(2,1)}, bf16[1,1,128,256]{3,2,1,0:T(8,128)(2,1)}, u32[]{:S(2)}, u32[]{:S(2)}) collective-permute-start(bf16[1,1,128,256]{3,2,1,0:T(8,128)(2,1)} %get-tuple-element.60), channel_id=1, source_target_pairs={{0,1},{1,2},{2,3},{3,4},{4,5},{5,6},{6,7},{8,9},{9,10},{10,11},{11... | collective-permute-start | bytes 196616 | tf_op jit(solution)/shard_map/ppermute | solution.py:28
  32.2 15.3 %collective-permute-start.1 = (bf16[1,1,128,256]{3,2,1,0:T(8,128)(2,1)}, bf16[1,1,128,256]{3,2,1,0:T(8,128)(2,1)}, u32[]{:S(2)}, u32[]{:S(2)}) collective-permute-start(bf16[1,1,128,256]{3,2,1,0:T(8,128)(2,1)} %get-tuple-element.61), channel_id=1, source_target_pairs={{1,0},{2,1},{3,2},{4,3},{5,4},{6,5},{7,6},{9,8},{10,9},{11,10},{12... | collective-permute-start | bytes 196616 | tf_op jit(solution)/shard_map/ppermute | solution.py:30
  33.5 1.3 copy-start.22
  33.5 1.2 copy-start.24
  39.3 1.9 copy-start.27
  50.5 1.9 copy-start.26
  57.1 3.1 %copy-start.10 = (bf16[16,8,17,256]{3,1,2,0:T(8,128)(2,1)}, bf16[16,8,17,256]{3,1,2,0:T(8,128)(2,1)S(1)}, u32[]{:S(2)}) copy-start(bf16[16,8,17,256]{3,1,2,0:T(8,128)(2,1)S(1)} %multiply_convert_fusion) | copy-start | bytes 3342340
  57.1 1.6 copy-start.3
  57.4 2.9 %copy-start.11 = (bf16[1,18,128,256]{2,3,1,0:T(8,128)(2,1)S(1)}, bf16[1,18,128,256]{2,3,1,0:T(8,128)(2,1)}, u32[]{:S(2)}) copy-start(bf16[1,18,128,256]{2,3,1,0:T(8,128)(2,1)} %get-tuple-element.54) | copy-start | bytes 3538948
  58.8 9.2 %copy-start.6 = (bf16[16,1,128,256]{3,0,2,1:T(8,128)(2,1)}, bf16[16,1,128,256]{3,0,2,1:T(8,128)(2,1)S(1)}, u32[]{:S(2)}) copy-start(bf16[16,1,128,256]{3,0,2,1:T(8,128)(2,1)S(1)} %slice.133) | copy-start | bytes 3145732
  67.9 1.6 copy-start.5
  69.5 3.0 %copy-start.12 = (bf16[1,8,17,256]{3,1,2,0:T(8,128)(2,1)S(1)}, bf16[1,8,17,256]{3,1,2,0:T(8,128)(2,1)}, u32[]{:S(2)}) copy-start(bf16[1,8,17,256]{3,1,2,0:T(8,128)(2,1)} %get-tuple-element.56) | copy-start | bytes 208900
  73.3 9.9 %collective-permute-start.6 = (bf16[1,1,128,256]{2,3,1,0:T(8,128)(2,1)}, bf16[1,1,128,256]{2,3,1,0:T(8,128)(2,1)}, u32[]{:S(2)}, u32[]{:S(2)}) collective-permute-start(bf16[1,1,128,256]{2,3,1,0:T(8,128)(2,1)} %copy.59), channel_id=1, source_target_pairs={{0,1},{1,2},{2,3},{3,4},{4,5},{5,6},{6,7},{8,9},{9,10},{10,11},{11... | collective-permute-start | bytes 196616 | tf_op jit(solution)/shard_map/ppermute | solution.py:28
  77.1 2.1 copy-start.25
  77.3 1.9 copy-start.4
  77.3 1.9 copy-start.7
  77.3 5.9 %collective-permute-start.7 = (bf16[1,1,128,256]{2,3,1,0:T(8,128)(2,1)S(1)}, bf16[1,1,128,256]{2,3,1,0:T(8,128)(2,1)S(1)}, u32[]{:S(2)}, u32[]{:S(2)}) collective-permute-start(bf16[1,1,128,256]{2,3,1,0:T(8,128)(2,1)S(1)} %copy.61), channel_id=1, source_target_pairs={{1,0},{2,1},{3,2},{4,3},{5,4},{6,5},{7,6},{9,8},{10,9},{11,10},{12... | collective-permute-start | bytes 196616 | tf_op jit(solution)/shard_map/ppermute | solution.py:30
  79.2 1.0 copy-start.18
  79.2 1.0 copy-start.19
  79.2 1.1 copy-start.23
  80.3 0.9 copy-start.13
  80.3 1.0 copy-start.14
  80.3 1.1 copy-start.15
  80.3 1.2 copy-start.16
  80.3 1.3 copy-start.17
  92.0 8.7 %copy-start.8 = (bf16[16,1,128,256]{3,0,2,1:T(8,128)(2,1)S(1)}, bf16[16,1,128,256]{3,0,2,1:T(8,128)(2,1)}, u32[]{:S(2)}) copy-start(bf16[16,1,128,256]{3,0,2,1:T(8,128)(2,1)} %copy-done.6) | copy-start | bytes 3145732
  93.8 7.4 %collective-permute-start.4 = (bf16[1,1,128,256]{3,2,1,0:T(8,128)(2,1)}, bf16[1,1,128,256]{3,2,1,0:T(8,128)(2,1)S(1)}, u32[]{:S(2)}, u32[]{:S(2)}) collective-permute-start(bf16[1,1,128,256]{3,2,1,0:T(8,128)(2,1)} %slice.132), channel_id=1, source_target_pairs={{0,1},{1,2},{2,3},{3,4},{4,5},{5,6},{6,7},{8,9},{9,10},{10,11},{11... | collective-permute-start | bytes 196616 | tf_op jit(solution)/shard_map/ppermute | solution.py:28
  98.1 4.6 %collective-permute-start.5 = (bf16[1,1,128,256]{3,2,1,0:T(8,128)(2,1)}, bf16[1,1,128,256]{3,2,1,0:T(8,128)(2,1)S(1)}, u32[]{:S(2)}, u32[]{:S(2)}) collective-permute-start(bf16[1,1,128,256]{3,2,1,0:T(8,128)(2,1)} %slice.135), channel_id=1, source_target_pairs={{1,0},{2,1},{3,2},{4,3},{5,4},{6,5},{7,6},{9,8},{10,9},{11,10},{12... | collective-permute-start | bytes 196616 | tf_op jit(solution)/shard_map/ppermute | solution.py:30
  112.5 2.0 copy-start.21
  238.4 3.4 %copy-start.9 = (f32[3,3,256,256]{3,2,1,0:T(8,128)S(1)}, f32[3,3,256,256]{3,2,1,0:T(8,128)}, u32[]{:S(2)}) copy-start(f32[3,3,256,256]{3,2,1,0:T(8,128)} %get-tuple-element.119) | copy-start | bytes 7077892
Sparse Core Ops, SparseCore 0:
  92.2 146.1 all-reduce.4
where the time goes:
time: 251 us; the launch traced here: 250 us
  waiting for transfers between devices  77.7 us (31%)
  blocking collectives  56.1 us (22%)
  local copies, waits for them, and re-layouts  40.5 us (16%)
  matrix products  29.5 us (12%)
  starting transfers between devices  18.6 us (7%)
  between operations  14.7 us (6%)
  other arithmetic  12.8 us (5%)
    psum x1, waiting for transfers between devices, body(): lax.psum((first_term, second_term, embed_term), ('dp', 'space'))  76.1 us
    psum x1, blocking collectives, body(): lax.psum((first_term, second_term, embed_term), ('dp', 'space'))  42.8 us
    unnamed x67, local copies, waits for them, and re-layouts  18.6 us
    dot_general x18, matrix products, kernel_grad(): jnp.dot(window.T, flat_grad, preferred_element_type=jnp.float32)  17.4 us
    all_gather x1, blocking collectives, prefix(): gathered = lax.all_gather(part, axis)  13.4 us
    ppermute x4, starting transfers between devices, padded_2(): lax.ppermute(tail, axis, [(i, (i + 1) % count) for i in range(ends)])  13.3 us
    conv_general_dilated x3, matrix products, convolve(): lax.conv_general_dilated(padded, kernel, (1, 1), ((0, 0), (1, 1)), dimens...  12.1 us
    conv_general_dilated x11, local copies, waits for them, and re-layouts, convolve(): lax.conv_general_dilated(padded, kernel, (1, 1), ((0, 0), (1, 1)), dimens...  11.5 us
  transfers between devices with their start and end apart: 9, of which 2 were waited for; matrix products, arithmetic and copies ran while one was open for 16% of the time, Pallas kernels for 0%

commit v1 on v0

v1 whole, which is shorter than its diff:
```python
import functools
import math

import jax
import jax.numpy as jnp
from jax import lax
from jax.experimental import pallas as pl
from jax.experimental.pallas import tpu as pltpu
from jax.sharding import PartitionSpec as P

MESH = pl.DeviceIdType.MESH
F32 = jnp.float32
BF16 = jnp.bfloat16


def each(count, step):
    if count <= 4:
        for k in range(1, count):
            step(k)
    else:

        def one(k, carry):
            step(k)
            return carry

        lax.fori_loop(1, count, one, 0)


class Exchange:
    def __init__(self, count, make):
        self.count, self.make = count, make

    def start(self):
        each(self.count, lambda k: self.make(k, True).start())

    def wait_recv(self):
        each(self.count, lambda k: self.make(k, False).wait_recv())

    def wait_send(self):
        each(self.count, lambda k: self.make(k, True).wait_send())


class Reduction:
    def __init__(self, place, scale, bufs, sems):
        self.dp, self.space, self.dp_count, self.outer_count = place
        self.core, self.outer = lax.rem(self.space, 2), lax.div(self.space, 2)
        self.full, self.half, self.r1, self.h32, self.h16, self.r2, self.q32, self.q16, self.r3, self.out = bufs
        self.scale = scale
        rows = self.full.shape[1]
        self.quarter = rows // self.dp_count
        self.split = self.quarter % (16 * self.outer_count) == 0
        self.part = self.quarter // self.outer_count if self.split else self.quarter
        pair_s, pair_r, dp_s, dp_r, out_s, out_r, gout_s, gout_r, gdp_s, gdp_r, gpair_s, gpair_r = sems
        core, dp, outer, quarter = self.core, self.dp, self.outer, self.quarter
        sibling = (dp, outer * 2 + 1 - core)

        def rows_of(index, size):
            return pl.ds(pl.multiple_of(index * size, 16), size)

        self.rows_of = rows_of
        make = pltpu.make_async_remote_copy

        def dp_at(k, to):
            return lax.rem(dp + (k if to else self.dp_count - k), self.dp_count)

        def outer_at(k, to):
            return lax.rem(outer + (k if to else self.outer_count - k), self.outer_count)

        def dp_id(k):
            return (dp_at(k, True), self.space)

        def outer_id(k):
            return (dp, outer_at(k, True) * 2 + core)

        def spot(o):
            start = dp * quarter + (o * self.part if self.split else 0)
            return pl.ds(pl.multiple_of(start, 16), self.part)

        self.spot = spot
        self.dp_at = dp_at
        self.s1 = Exchange(2, lambda k, to: make(self.half.at[1 - core], self.r1, pair_s.at[0], pair_r.at[0], device_id=sibling, device_id_type=MESH))
        self.s2_make = lambda k, to: make(
            self.h16.at[rows_of(dp_at(k, True), quarter)], self.r2.at[k - 1], dp_s.at[k - 1], dp_r.at[k - 1], device_id=dp_id(k), device_id_type=MESH
        )
        self.s2 = Exchange(self.dp_count, self.s2_make)
        if self.split:
            self.s3 = Exchange(
                self.outer_count,
                lambda k, to: make(
                    self.q16.at[rows_of(outer_at(k, True), self.part)], self.r3.at[k - 1], out_s.at[k - 1], out_r.at[k - 1], device_id=outer_id(k), device_id_type=MESH
                ),
            )
            self.g3 = Exchange(
                self.outer_count,
                lambda k, to: make(
                    self.out.at[core, spot(outer)],
                    self.out.at[core, spot(outer if to else outer_at(k, False))],
                    gout_s.at[k - 1], gout_r.at[k - 1], device_id=outer_id(k), device_id_type=MESH,
                ),
            )
        else:
            self.s3 = Exchange(
                self.outer_count,
                lambda k, to: make(
                    self.q16, self.r3.at[outer if to else outer_at(k, False)], out_s.at[k - 1], out_r.at[k - 1], device_id=outer_id(k), device_id_type=MESH
                ),
            )
            self.g3 = None
        self.g2 = Exchange(
            self.dp_count,
            lambda k, to: make(
                self.out.at[core, rows_of(dp, quarter)],
                self.out.at[core, rows_of(dp if to else dp_at(k, False), quarter)],
                gdp_s.at[k - 1], gdp_r.at[k - 1], device_id=dp_id(k), device_id_type=MESH,
            ),
        )
        self.g1 = Exchange(
            2,
            lambda k, to: make(
                self.out.at[core], self.out.at[core if to else 1 - core], gpair_s.at[0], gpair_r.at[0], device_id=sibling, device_id_type=MESH
            ),
        )

    def start(self):
        self.s1.start()

    def pair_to_dp(self):
        self.s1.wait_recv()

        def total(index):
            where = self.rows_of(index, self.quarter)
            value = self.full[self.core, where, :] + self.r1[where, :].astype(F32)
            return where, value

        for k in range(1, self.dp_count):
            where, value = total(self.dp_at(k, True))
            self.h16[where, :] = value.astype(BF16)
            self.s2_make(k, True).start()
        _, value = total(self.dp)
        self.h32[...] = value

    def dp_to_outer(self):
        self.s2.wait_recv()
        value = self.h32[...]
        for k in range(1, self.dp_count):
            value = value + self.r2[k - 1].astype(F32)
        self.q32[...] = value
        self.q16[...] = value.astype(BF16)
        self.s3.start()

    def outer_to_gather(self):
        self.s3.wait_recv()
        if self.split:
            value = self.q32[self.rows_of(self.outer, self.part), :]
            for k in range(1, self.outer_count):
                value = value + self.r3[k - 1].astype(F32)
            self.out[self.core, self.spot(self.outer), :] = (value * self.scale).astype(BF16)
            self.g3.start()
        else:
            self.r3[self.outer] = self.q16[...]
            value = lax.fori_loop(0, self.outer_count, lambda j, v: v + self.r3[j].astype(F32), jnp.zeros(self.q32.shape, F32))
            self.out[self.core, self.spot(self.outer), :] = (value * self.scale).astype(BF16)

    def gather_dp(self):
        if self.g3 is not None:
            self.g3.wait_recv()
        self.g2.start()

    def gather_pair(self):
        self.g2.wait_recv()
        self.g1.start()

    def finish(self):
        self.g1.wait_recv()
        for phase in (self.s1, self.s2, self.s3, self.g3, self.g2, self.g1):
            if phase is not None:
                phase.wait_send()


def put(cat, at, value, edge):
    count, width = value.shape
    rows = pl.ds(at, count)
    cat[rows, width : 2 * width] = value.astype(BF16)
    cat[rows, 0:width] = jnp.where(edge == 0, 0.0, pltpu.roll(value, 1, 0)).astype(BF16)
    cat[rows, 2 * width :] = jnp.where(edge == count - 1, 0.0, pltpu.roll(value, count - 1, 0)).astype(BF16)


def kernel(counts, scale, decline, feat, high, cot, w1, w2, embed, gfeat, out1, out2, eout, *scratch):
    dp_count, space_count = counts
    (
        stat, stats, halo_f, halo_c, halo_h, edge_h, shade, wide_shade, xcat, ccat, hcat, xt, at, slope,
        full1, half1, r11, h321, h161, r21, q321, q161, r31,
        full2, half2, r12, h322, h162, r22, q322, q162, r32,
        esum, edp, esp,
        halo_s, halo_r, stat_s, stat_r, edp_s, edp_r, esp_s, esp_r,
    ) = scratch[:43]
    sems1, sems2 = scratch[43:55], scratch[55:67]
    dp, space = lax.axis_index("dp"), lax.axis_index("space")
    strip, cols = high.shape
    width = feat.shape[1]
    pixels = strip * cols
    last = space_count - 1
    make = pltpu.make_async_remote_copy

    barrier = pltpu.get_barrier_semaphore()
    each(dp_count, lambda k: pl.semaphore_signal(barrier, inc=1, device_id=(lax.rem(dp + k, dp_count), space), device_id_type=MESH))
    each(space_count, lambda k: pl.semaphore_signal(barrier, inc=1, device_id=(dp, lax.rem(space + k, space_count)), device_id_type=MESH))

    row_at = lax.broadcasted_iota(jnp.int32, (strip, cols), 0)
    lifted = high[...] + decline * (space * strip + row_at).astype(F32)
    peak = jnp.max(lifted, axis=0, keepdims=True)
    stat[...] = jnp.zeros_like(stat)
    stat[0:1, :] = peak
    stat[1:2, :] = jnp.max(lifted[: strip - 1], axis=0, keepdims=True)
    stat[2:3, :] = lifted[strip - 1 :]
    stat[3:4, :] = lifted[:1]
    pl.semaphore_wait(barrier, dp_count + space_count - 2)

    up = (dp, lax.rem(space + last, space_count))
    down = (dp, lax.rem(space + 1, space_count))
    peaks = Exchange(
        space_count,
        lambda k, to: make(stat, stats.at[k - 1], stat_s.at[k - 1], stat_r.at[k - 1], device_id=(dp, lax.rem(space + k, space_count)), device_id_type=MESH),
    )
    peaks.start()
    tail = pl.ds(pixels - cols, cols)
    sides = []
    for at_sem, (source, halo) in enumerate(((feat, halo_f), (cot, halo_c))):
        sides.append(make(source.at[tail], halo.at[0], halo_s.at[2 * at_sem], halo_r.at[2 * at_sem], device_id=down, device_id_type=MESH))
        sides.append(make(source.at[pl.ds(0, cols)], halo.at[1], halo_s.at[2 * at_sem + 1], halo_r.at[2 * at_sem + 1], device_id=up, device_id_type=MESH))
    for copy in sides:
        copy.start()

    edge = lax.broadcasted_iota(jnp.int32, (cols, width), 0)

    def cot_row(r, carry):
        value = cot[pl.ds(pl.multiple_of(r * cols, cols), cols), :].astype(F32)
        put(ccat, pl.multiple_of((r + 1) * cols, cols), value, edge)
        return carry

    lax.fori_loop(0, strip, cot_row, 0)
    for offset in range(3):
        place = pl.ds(offset * width, width)
        for gap in (((2 - offset) + strip) % (strip + 2), ((2 - offset) + strip + 1) % (strip + 2)):
            at[place, pl.ds(gap * cols, cols)] = jnp.zeros((width, cols), BF16)

    peaks.wait_recv()
    zero = jnp.zeros((1, cols), F32)

    def carry_peak(k, carried):
        return jnp.maximum(carried, jnp.where(k <= space, stats[k - 1, 0:1, :], zero))

    above = lax.fori_loop(2, space_count, carry_peak, zero)
    carried = carry_peak(1, above)
    shade[...] = jnp.zeros_like(shade)
    shade[0:1, :] = jnp.maximum(jnp.maximum(above, stats[0, 1:2, :]) - stats[0, 2:3, :], 0.0)
    running = carried
    for r in range(strip):
        shade[r + 1 : r + 2, :] = jnp.maximum(running - lifted[r : r + 1], 0.0)
        running = jnp.maximum(running, lifted[r : r + 1])
    shade[strip + 1 : strip + 2, :] = jnp.maximum(running - stats[last - 1, 3:4, :], 0.0)
    turned = shade[...].T
    direction = embed[...].astype(F32)

    for copy in sides:
        copy.wait_recv()
    inside = (space > 0, space < last)
    for side, p in ((0, 0), (1, strip + 1)):
        put(ccat, p * cols, jnp.where(inside[side], halo_c[side].astype(F32), 0.0), edge)

    for p in range(strip + 2):
        column = jnp.broadcast_to(turned[:, p : p + 1], (cols, 128))
        if 1 <= p <= strip:
            wide_shade[pl.ds((p - 1) * cols, cols), :] = column
            value = feat[pl.ds((p - 1) * cols, cols), :].astype(F32)
        else:
            value = halo_f[0 if p == 0 else 1].astype(F32)
        value = value + jnp.concatenate([column] * (width // 128), axis=1) * direction
        if p in (0, strip + 1):
            value = jnp.where(inside[0 if p == 0 else 1], value, 0.0)
        put(xcat, p * cols, value, edge)
        flipped = value.astype(BF16).T
        for offset in range(3):
            if 0 <= p - offset < strip:
                xt[pl.ds(offset * width, width), pl.ds((p - offset) * cols, cols)] = flipped

    block = 4
    size = block * cols

    def blocks(step):
        def one(i, carry):
            step(i)
            return carry

        lax.fori_loop(0, strip // block, one, 0)

    def rows(i, shift=0):
        return pl.ds(pl.multiple_of(i * size + shift * cols, cols), size)

    def forward(i):
        total = jnp.zeros((size, width), F32)
        for a in range(3):
            total += jnp.dot(xcat[rows(i, a), :], w1[pl.ds(a * 3 * width, 3 * width), :], preferred_element_type=F32)
        sigma = jax.nn.sigmoid(total)
        slope[rows(i), :] = sigma * (1.0 + total * (1.0 - sigma))
        flipped = (total * sigma).astype(BF16).T
        for a in range(3):
            at[pl.ds(a * width, width), pl.ds(pl.multiple_of(i * size + (2 - a) * cols, cols), size)] = flipped

    def backward(i, cat, weight):
        total = jnp.zeros((size, width), F32)
        for a in range(3):
            for b in range(3):
                total += lax.dot_general(
                    cat[rows(i, a), b * width : (b + 1) * width],
                    weight[pl.ds(((2 - a) * 3 + 2 - b) * width, width), :],
                    (((1,), (1,)), ((), ())),
                    preferred_element_type=F32,
                )
        return total

    def kernel_grad(left, cat, first, count, full, half):
        def one(b, carry):
            value = jnp.dot(
                left[...], cat[pl.ds(first, count), pl.ds(pl.multiple_of((2 - b) * width, width), width)], preferred_element_type=F32
            )
            for a in range(3):
                for side in range(2):
                    piece = value[a * width : (a + 1) * width, side * (width // 2) : (side + 1) * (width // 2)]
                    where = pl.ds(pl.multiple_of((a * 3 + b) * width, width), width)
                    full[side, where, :] = piece
                    half[side, where, :] = piece.astype(BF16)
            return carry

        lax.fori_loop(0, 3, one, 0)

    place = (dp, space, dp_count, space_count // 2)
    first = Reduction(place, scale, (full1, half1, r11, h321, h161, r21, q321, q161, r31, out1), sems1)
    second = Reduction(place, scale, (full2, half2, r12, h322, h162, r22, q322, q162, r32, out2), sems2)

    blocks(forward)
    kernel_grad(at, ccat, 0, (strip + 2) * cols, full2, half2)
    second.start()

    def hidden(i):
        value = backward(i, ccat, w2) * slope[rows(i), :]
        for j in range(block):
            put(hcat, pl.multiple_of(i * size + (j + 1) * cols, cols), value[j * cols : (j + 1) * cols], edge)

    blocks(hidden)
    edge_h[0] = hcat[pl.ds(strip * cols, cols), width : 2 * width]
    edge_h[1] = hcat[pl.ds(cols, cols), width : 2 * width]
    borders = [
        make(edge_h.at[0], halo_h.at[0], halo_s.at[4], halo_r.at[4], device_id=down, device_id_type=MESH),
        make(edge_h.at[1], halo_h.at[1], halo_s.at[5], halo_r.at[5], device_id=up, device_id_type=MESH),
    ]
    for copy in borders:
        copy.start()
    second.pair_to_dp()
    kernel_grad(xt, hcat, cols, pixels, full1, half1)
    first.start()
    for copy in borders:
        copy.wait_recv()
    for side, p in ((0, 0), (1, strip + 1)):
        put(hcat, p * cols, jnp.where(inside[side], halo_h[side].astype(F32), 0.0), edge)
    first.pair_to_dp()
    esum[...] = jnp.zeros_like(esum)

    def inputs(i):
        value = backward(i, hcat, w1)
        gfeat[rows(i), :] = (cot[rows(i), :].astype(F32) + value).astype(BF16)
        lean = wide_shade[rows(i), :]
        weighted = jnp.concatenate([lean] * (width // 128), axis=1) * value
        esum[...] += jnp.sum(weighted.reshape(size // 8, 8, width), axis=0)

    blocks(inputs)
    edp[dp] = esum[...]
    share_dp = Exchange(
        dp_count,
        lambda k, to: make(
            esum, edp.at[dp if to else lax.rem(dp + dp_count - k, dp_count)], edp_s.at[k - 1], edp_r.at[k - 1],
            device_id=(lax.rem(dp + k, dp_count), space), device_id_type=MESH,
        ),
    )
    share_dp.start()
    second.dp_to_outer()
    share_dp.wait_recv()
    value = edp[0]
    for k in range(1, dp_count):
        value = value + edp[k]
    esp[space] = value
    share_space = Exchange(
        space_count,
        lambda k, to: make(
            esp.at[space], esp.at[space if to else lax.rem(space + space_count - k, space_count)], esp_s.at[k - 1], esp_r.at[k - 1],
            device_id=(dp, lax.rem(space + k, space_count)), device_id_type=MESH,
        ),
    )
    share_space.start()
    second.outer_to_gather()
    first.dp_to_outer()
    second.gather_dp()
    first.outer_to_gather()
    share_space.wait_recv()
    value = lax.fori_loop(1, space_count, lambda k, v: v + esp[k], esp[0])
    eout[...] = jnp.sum(value, axis=0, keepdims=True) * scale
    first.gather_dp()
    second.gather_pair()
    first.gather_pair()
    for copy in sides + borders:
        copy.wait_send()
    peaks.wait_send()
    share_dp.wait_send()
    share_space.wait_send()
    second.finish()
    first.finish()


def body(features, heights, cotangent, weight_first, weight_second, shade_embed):
    images, strip, cols, width = features.shape
    dp_count, space_count = lax.axis_size("dp"), lax.axis_size("space")
    total_rows = strip * space_count
    outer = space_count // 2
    scale = 1.0 / math.sqrt(images * dp_count * total_rows * cols)
    pixels = strip * cols
    halo = (strip + 2) * cols
    taps = 9 * width
    lanes = width // 2
    quarter = taps // dp_count
    split = quarter % (16 * outer) == 0
    vmem = pltpu.VMEM
    dma = pltpu.SemaphoreType.DMA
    r3 = (outer - 1, quarter // outer, lanes) if split else (outer, quarter, lanes)
    reduction = [
        vmem((2, taps, lanes), F32), vmem((2, taps, lanes), BF16), vmem((taps, lanes), BF16),
        vmem((quarter, lanes), F32), vmem((taps, lanes), BF16), vmem((dp_count - 1, quarter, lanes), BF16),
        vmem((quarter, lanes), F32), vmem((quarter, lanes), BF16), vmem(r3, BF16),
    ]
    pairs = [1, dp_count - 1, outer - 1, outer - 1, dp_count - 1, 1]
    phase_sems = [dma((count,)) for count in pairs for _ in range(2)]
    scratch = [
        vmem((8, cols), F32), vmem((space_count - 1, 8, cols), F32),
        vmem((2, cols, width), BF16), vmem((2, cols, width), BF16), vmem((2, cols, width), BF16), vmem((2, cols, width), BF16),
        vmem((128, cols), F32), vmem((pixels, 128), F32),
        vmem((halo, 3 * width), BF16), vmem((halo, 3 * width), BF16), vmem((halo, 3 * width), BF16),
        vmem((3 * width, pixels), BF16), vmem((3 * width, halo), BF16), vmem((pixels, width), F32),
        *reduction, *reduction,
        vmem((8, width), F32), vmem((dp_count, 8, width), F32), vmem((space_count, 8, width), F32),
        dma((6,)), dma((6,)), dma((space_count - 1,)), dma((space_count - 1,)),
        dma((dp_count - 1,)), dma((dp_count - 1,)), dma((space_count - 1,)), dma((space_count - 1,)),
        *phase_sems, *phase_sems,
    ]
    spec = pl.BlockSpec(memory_space=pltpu.VMEM)
    gfeat, first, second, total = pl.pallas_call(
        functools.partial(kernel, (dp_count, space_count), scale, 2.0 / total_rows),
        out_shape=(
            jax.ShapeDtypeStruct((pixels, width), BF16),
            jax.ShapeDtypeStruct((2, taps, lanes), BF16),
            jax.ShapeDtypeStruct((2, taps, lanes), BF16),
            jax.ShapeDtypeStruct((1, width), F32),
        ),
        in_specs=[spec] * 6,
        out_specs=(spec,) * 4,
        scratch_shapes=scratch,
        compiler_params=pltpu.CompilerParams(collective_id=0, has_side_effects=True, vmem_limit_bytes=60 * 2**20),
        cost_estimate=pl.CostEstimate(flops=90 * pixels * width * width, bytes_accessed=2**24, transcendentals=pixels * width),
    )(
        features.reshape(pixels, width),
        heights.reshape(strip, cols),
        cotangent.reshape(pixels, width),
        weight_first.reshape(taps, width),
        weight_second.reshape(taps, width),
        shade_embed.reshape(1, width),
    )

    def joined(halves):
        return jnp.concatenate([halves[0], halves[1]], axis=1).astype(F32).reshape(3, 3, width, width)

    return gfeat.reshape(features.shape), joined(first), joined(second), total.reshape(width)


def solution(mesh):
    in_specs = (
        P("dp", "space", None, None),
        P("dp", "space", None),
        P("dp", "space", None, None),
        P(),
        P(),
        P(),
    )
    out_specs = (P("dp", "space", None, None), P(), P(), P())
    return jax.shard_map(body, mesh=mesh, in_specs=in_specs, out_specs=out_specs, check_vma=False)
```

time: 251 us -> 73.4 us (0.29)
  waiting for transfers between devices: 77.7 us -> 0 us
  Pallas kernels: 0 us -> 64.9 us
  blocking collectives: 56.1 us -> 0 us
  local copies, waits for them, and re-layouts: 40.5 us -> 4.52 us
  matrix products: 29.5 us -> 0 us
  starting transfers between devices: 18.6 us -> 0 us
  between operations: 14.7 us -> 0.65 us
  other arithmetic: 12.8 us -> 3.14 us
    psum x1 -> x0, waiting for transfers between devices: 76.1 us -> none  [body(): lax.psum((first_term, second_term, embed_term), ('dp', 'space'))]
    pallas_call x0 -> x1, Pallas kernels: none -> 64.9 us  [body(): pl.pallas_call(functools.partial(kernel, (dp_count, space_count), scale,...]
    psum x1 -> x0, blocking collectives: 42.8 us -> none  [body(): lax.psum((first_term, second_term, embed_term), ('dp', 'space'))]
    ppermute x8 -> x0, starting transfers between devices: 18.6 us -> none  [the longest x4 13.3 us: padded_2(): lax.ppermute(tail, axis, [(i, (i + 1) % count) for i in range(ends)])]
    dot_general x18 -> x0, matrix products: 17.4 us -> none  [kernel_grad(): jnp.dot(window.T, flat_grad, preferred_element_type=jnp.float32)]
    unnamed x67 -> x6, local copies, waits for them, and re-layouts: 18.6 us -> 1.54 us
    all_gather x1 -> x0, blocking collectives: 13.4 us -> none  [prefix(): gathered = lax.all_gather(part, axis)]
    conv_general_dilated x3 -> x0, matrix products: 12.1 us -> none  [convolve(): lax.conv_general_dilated(padded, kernel, (1, 1), ((0, 0), (1, 1)), dimens...]
  transfers between devices with their start and end apart: 9 -> 0, of which waited for: 2 -> 0; matrix products, arithmetic and copies ran while one was open for 16% -> 0% of each run, Pallas kernels for 0% -> 0%
where the time goes in v1:
time: 73.4 us; the launch traced here: 73.2 us
  Pallas kernels  64.9 us (88%)
  local copies, waits for them, and re-layouts  4.52 us (6%)
  other arithmetic  3.14 us (4%)
    pallas_call x1, Pallas kernels, body(): pl.pallas_call(functools.partial(kernel, (dp_count, space_count), scale,...  64.9 us
    convert_element_type x2, other arithmetic, joined(): jnp.concatenate([halves[0], halves[1]], axis=1).astype(F32)  3.14 us
    slice x1, local copies, waits for them, and re-layouts, joined(): halves[0]  1.75 us
    unnamed x6, local copies, waits for them, and re-layouts  1.54 us

profile of v1, /device:TPU:0, one launch (start us, length us, event | category | flops | bytes accessed | tf_op | source)
XLA Modules:
  0.0 73.2 jit_solution(6130432981065200105)
XLA Ops:
  0.6 1.2 %reshape.47.embed = bf16[1,256]{1,0:T(2,128)(2,1)} reshape(bf16[256]{0:T(256)(128)(2,1)} %param.11) | data formatting | bytes 1024 | tf_op jit(solution)/shard_map/reshape | solution.py:473
  1.9 64.9 %shard_map.93 = (bf16[2048,256]{1,0:T(8,128)(2,1)}, bf16[2,2304,128]{2,1,0:T(8,128)(2,1)}, bf16[2,2304,128]{2,1,0:T(8,128)(2,1)}, f32[1,256]{1,0:T(1,128)}) custom-call(bf16[2048,256]{1,0:T(8,128)(2,1)} %bitcast.19, f32[16,128]{1,0:T(8,128)} %bitcast.21, bf16[2048,256]{1,0:T(8,128)(2,1)} %bitcast.20, bf16[2304,256]{1,0:T(8,128)(2,1)} %bitcast.17, ...), custom_call_target="tpu_custom_call" | custom-call | flops 12079595520 | bytes 16777216 | tf_op jit(solution)/shard_map/pallas_call | solution.py:454
  66.8 1.8 %fusion = (bf16[1,2304,128]{2,1,0:T(8,128)(2,1)S(1)}, bf16[1,2304,128]{2,1,0:T(8,128)(2,1)S(1)}, bf16[1,2304,128]{2,1,0:T(8,128)(2,1)S(1)}, bf16[1,2304,128]{2,1,0:T(8,128)(2,1)S(1)}) fusion(bf16[2,2304,128]{2,1,0:T(8,128)(2,1)} %get-tuple-element.10, bf16[2,2304,128]{2,1,0:T(8,128)(2,1)} %get-tuple-element.9), kind=kLoop, calls=%fused_computation.2 | loop fusion | bytes 4718592 | tf_op jit(solution)/shard_map/slice | solution.py:477
  68.5 1.6 %maximum_convert_fusion.1 = f32[3,3,256,256]{3,2,1,0:T(8,128)} fusion(bf16[3,3,256,128]{3,2,1,0:T(8,128)(2,1)S(1)} %bitcast.14, bf16[3,3,256,128]{3,2,1,0:T(8,128)(2,1)S(1)} %bitcast.13), kind=kLoop, calls=%fused_computation.1 | loop fusion | flops 2359296 | bytes 3538944 | tf_op jit(solution)/shard_map/convert_element_type | solution.py:477
  70.1 0.0 copy-start
  70.1 0.0 copy-start.1
  70.1 1.6 %maximum_convert_fusion = f32[3,3,256,256]{3,2,1,0:T(8,128)} fusion(bf16[3,3,256,128]{3,2,1,0:T(8,128)(2,1)S(1)} %bitcast.11, bf16[3,3,256,128]{3,2,1,0:T(8,128)(2,1)S(1)} %bitcast.12), kind=kLoop, calls=%fused_computation | loop fusion | flops 2359296 | bytes 3538944 | tf_op jit(solution)/shard_map/convert_element_type | solution.py:477
  71.7 0.0 copy-done
  71.7 1.0 %copy.12 = bf16[1,16,128,256]{3,2,1,0:T(8,128)(2,1)} copy(bf16[1,16,128,256]{3,2,1,0:T(8,128)(2,1)S(1)} %bitcast.15) | data formatting | bytes 2097152
  72.6 0.0 copy-done.1
  72.6 0.6 copy.13
Async XLA Ops:
  70.1 1.6 %copy-start = (bf16[2048,256]{1,0:T(8,128)(2,1)S(1)}, bf16[2048,256]{1,0:T(8,128)(2,1)}, u32[]{:S(2)}) copy-start(bf16[2048,256]{1,0:T(8,128)(2,1)} %get-tuple-element.8) | copy-start | bytes 3145732
  70.1 2.5 %copy-start.1 = (f32[1,256]{1,0:T(1,128)S(1)}, f32[1,256]{1,0:T(1,128)}, u32[]{:S(2)}) copy-start(f32[1,256]{1,0:T(1,128)} %get-tuple-element.11) | copy-start | bytes 3076

commit v2 on v1

--- a/solution.py
+++ b/solution.py
@@ -11,6 +11,8 @@
 MESH = pl.DeviceIdType.MESH
 F32 = jnp.float32
 BF16 = jnp.bfloat16
+PIECES = 3
+DELAYS = (1, 3, 6, 8, 11)
 
 
 def each(count, step):
@@ -41,12 +43,16 @@
 
 
 class Reduction:
-    def __init__(self, place, scale, bufs, sems):
+    def __init__(self, place, scale, base, bufs, sems):
         self.dp, self.space, self.dp_count, self.outer_count = place
         self.core, self.outer = lax.rem(self.space, 2), lax.div(self.space, 2)
         self.full, self.half, self.r1, self.h32, self.h16, self.r2, self.q32, self.q16, self.r3, self.out = bufs
+        self.base = base
         self.scale = scale
-        rows = self.full.shape[1]
+        rows, lanes = self.full.shape[1:]
+        mine = pl.ds(pl.multiple_of(self.core * lanes, lanes), lanes)
+        theirs = pl.ds(pl.multiple_of((1 - self.core) * lanes, lanes), lanes)
+        self.mine = mine
         self.quarter = rows // self.dp_count
         self.split = self.quarter % (16 * self.outer_count) == 0
         self.part = self.quarter // self.outer_count if self.split else self.quarter
@@ -54,8 +60,8 @@
         core, dp, outer, quarter = self.core, self.dp, self.outer, self.quarter
         sibling = (dp, outer * 2 + 1 - core)
 
-        def rows_of(index, size):
-            return pl.ds(pl.multiple_of(index * size, 16), size)
+        def rows_of(index, size, start=0):
+            return pl.ds(pl.multiple_of(start + index * size, 16), size)
 
         self.rows_of = rows_of
         make = pltpu.make_async_remote_copy
@@ -73,7 +79,7 @@
             return (dp, outer_at(k, True) * 2 + core)
 
         def spot(o):
-            start = dp * quarter + (o * self.part if self.split else 0)
+            start = base + dp * quarter + (o * self.part if self.split else 0)
             return pl.ds(pl.multiple_of(start, 16), self.part)
 
         self.spot = spot
@@ -93,8 +99,8 @@
             self.g3 = Exchange(
                 self.outer_count,
                 lambda k, to: make(
-                    self.out.at[core, spot(outer)],
-                    self.out.at[core, spot(outer if to else outer_at(k, False))],
+                    self.out.at[spot(outer), mine],
+                    self.out.at[spot(outer if to else outer_at(k, False)), mine],
                     gout_s.at[k - 1], gout_r.at[k - 1], device_id=outer_id(k), device_id_type=MESH,
                 ),
             )
@@ -109,15 +115,15 @@
         self.g2 = Exchange(
             self.dp_count,
             lambda k, to: make(
-                self.out.at[core, rows_of(dp, quarter)],
-                self.out.at[core, rows_of(dp if to else dp_at(k, False), quarter)],
+                self.out.at[rows_of(dp, quarter, base), mine],
+                self.out.at[rows_of(dp if to else dp_at(k, False), quarter, base), mine],
                 gdp_s.at[k - 1], gdp_r.at[k - 1], device_id=dp_id(k), device_id_type=MESH,
             ),
         )
         self.g1 = Exchange(
             2,
             lambda k, to: make(
-                self.out.at[core], self.out.at[core if to else 1 - core], gpair_s.at[0], gpair_r.at[0], device_id=sibling, device_id_type=MESH
+                self.out.at[pl.ds(base, rows), mine], self.out.at[pl.ds(base, rows), mine if to else theirs], gpair_s.at[0], gpair_r.at[0], device_id=sibling, device_id_type=MESH
             ),
         )
 
@@ -154,12 +160,12 @@
             value = self.q32[self.rows_of(self.outer, self.part), :]
             for k in range(1, self.outer_count):
                 value = value + self.r3[k - 1].astype(F32)
-            self.out[self.core, self.spot(self.outer), :] = (value * self.scale).astype(BF16)
+            self.out[self.spot(self.outer), self.mine] = (value * self.scale).astype(BF16)
             self.g3.start()
         else:
             self.r3[self.outer] = self.q16[...]
             value = lax.fori_loop(0, self.outer_count, lambda j, v: v + self.r3[j].astype(F32), jnp.zeros(self.q32.shape, F32))
-            self.out[self.core, self.spot(self.outer), :] = (value * self.scale).astype(BF16)
+            self.out[self.spot(self.outer), self.mine] = (value * self.scale).astype(BF16)
 
     def gather_dp(self):
         if self.g3 is not None:
@@ -188,13 +194,11 @@
 def kernel(counts, scale, decline, feat, high, cot, w1, w2, embed, gfeat, out1, out2, eout, *scratch):
     dp_count, space_count = counts
     (
-        stat, stats, halo_f, halo_c, halo_h, edge_h, shade, wide_shade, xcat, ccat, hcat, xt, at, slope,
-        full1, half1, r11, h321, h161, r21, q321, q161, r31,
-        full2, half2, r12, h322, h162, r22, q322, q162, r32,
+        stat, stats, halo_f, halo_c, halo_h, edge_h, shade, wide_shade, xcat, ccat, hcat, xt, at, back,
         esum, edp, esp,
         halo_s, halo_r, stat_s, stat_r, edp_s, edp_r, esp_s, esp_r,
-    ) = scratch[:43]
-    sems1, sems2 = scratch[43:55], scratch[55:67]
+    ) = scratch[:25]
+    groups, sems = scratch[25 : 25 + 18 * PIECES], scratch[25 + 18 * PIECES :]
     dp, space = lax.axis_index("dp"), lax.axis_index("space")
     strip, cols = high.shape
     width = feat.shape[1]
@@ -223,13 +227,36 @@
         lambda k, to: make(stat, stats.at[k - 1], stat_s.at[k - 1], stat_r.at[k - 1], device_id=(dp, lax.rem(space + k, space_count)), device_id_type=MESH),
     )
     peaks.start()
-    tail = pl.ds(pixels - cols, cols)
-    sides = []
-    for at_sem, (source, halo) in enumerate(((feat, halo_f), (cot, halo_c))):
-        sides.append(make(source.at[tail], halo.at[0], halo_s.at[2 * at_sem], halo_r.at[2 * at_sem], device_id=down, device_id_type=MESH))
-        sides.append(make(source.at[pl.ds(0, cols)], halo.at[1], halo_s.at[2 * at_sem + 1], halo_r.at[2 * at_sem + 1], device_id=up, device_id_type=MESH))
-    for copy in sides:
-        copy.start()
+    inside = (space > 0, space < last)
+
+    def sides_of(bottom, top, halo, at_sem):
+        return [
+            (space < last, space > 0, make(bottom, halo.at[0], halo_s.at[at_sem], halo_r.at[at_sem], device_id=down, device_id_type=MESH)),
+            (space > 0, space < last, make(top, halo.at[1], halo_s.at[at_sem + 1], halo_r.at[at_sem + 1], device_id=up, device_id_type=MESH)),
+        ]
+
+    def start_sides(copies):
+        for sends, _, copy in copies:
+            pl.when(sends)(copy.start)
+
+    def wait_sides(copies):
+        for _, gets, copy in copies:
+            pl.when(gets)(copy.wait_recv)
+
+    def end_sides(copies):
+        for sends, _, copy in copies:
+            pl.when(sends)(copy.wait_send)
+
+    tail, front = pl.ds(pixels - cols, cols), pl.ds(0, cols)
+    sides = sides_of(feat.at[tail], feat.at[front], halo_f, 0) + sides_of(cot.at[tail], cot.at[front], halo_c, 2)
+    for edge_halo in (halo_f, halo_c, halo_h):
+        for side in range(2):
+
+            @pl.when(jnp.logical_not(inside[side]))
+            def _():
+                edge_halo[side] = jnp.zeros((cols, width), BF16)
+
+    start_sides(sides)
 
     edge = lax.broadcasted_iota(jnp.int32, (cols, width), 0)
 
@@ -243,6 +270,36 @@
         place = pl.ds(offset * width, width)
         for gap in (((2 - offset) + strip) % (strip + 2), ((2 - offset) + strip + 1) % (strip + 2)):
             at[place, pl.ds(gap * cols, cols)] = jnp.zeros((width, cols), BF16)
+
+    block = 4
+    size = block * cols
+
+    def rows(i, shift=0):
+        return pl.ds(pl.multiple_of(i * size + shift * cols, cols), size)
+
+    def backward(i, cat, weight):
+        total = jnp.zeros((size, width), F32)
+        for a in range(3):
+            for b in range(3):
+                total += lax.dot_general(
+                    cat[rows(i, a), b * width : (b + 1) * width],
+                    weight[pl.ds(((2 - a) * 3 + 2 - b) * width, width), :],
+                    (((1,), (1,)), ((), ())),
+                    preferred_element_type=F32,
+                )
+        return total
+
+    def loop(start, stop, step):
+        def one(i, carry):
+            step(i)
+            return carry
+
+        lax.fori_loop(start, stop, one, 0)
+
+    def back_act(i):
+        back[rows(i), :] = backward(i, ccat, w2)
+
+    loop(1, strip // block - 1, back_act)
 
     peaks.wait_recv()
     zero = jnp.zeros((1, cols), F32)
@@ -260,13 +317,14 @@
         running = jnp.maximum(running, lifted[r : r + 1])
     shade[strip + 1 : strip + 2, :] = jnp.maximum(running - stats[last - 1, 3:4, :], 0.0)
     turned = shade[...].T
-    direction = embed[...].astype(F32)
-
-    for copy in sides:
-        copy.wait_recv()
-    inside = (space > 0, space < last)
+    direction = embed[...].astype(F32).reshape(1, width)
+
+    wait_sides(sides)
     for side, p in ((0, 0), (1, strip + 1)):
         put(ccat, p * cols, jnp.where(inside[side], halo_c[side].astype(F32), 0.0), edge)
+
+    back_act(0)
+    back_act(strip // block - 1)
 
     for p in range(strip + 2):
         column = jnp.broadcast_to(turned[:, p : p + 1], (cols, 128))
@@ -284,87 +342,24 @@
             if 0 <= p - offset < strip:
                 xt[pl.ds(offset * width, width), pl.ds((p - offset) * cols, cols)] = flipped
 
-    block = 4
-    size = block * cols
-
-    def blocks(step):
-        def one(i, carry):
-            step(i)
-            return carry
-
-        lax.fori_loop(0, strip // block, one, 0)
-
-    def rows(i, shift=0):
-        return pl.ds(pl.multiple_of(i * size + shift * cols, cols), size)
+    def kernel_grad(left, cat, first, count, b, full, half, row):
+        value = jnp.dot(left[...], cat[pl.ds(first, count), (2 - b) * width : (3 - b) * width], preferred_element_type=F32)
+        for side in range(2):
+            piece = value[:, side * (width // 2) : (side + 1) * (width // 2)]
+            full[side, pl.ds(row, 3 * width), :] = piece
+            half[side, pl.ds(row, 3 * width), :] = piece.astype(BF16)
 
     def forward(i):
         total = jnp.zeros((size, width), F32)
         for a in range(3):
             total += jnp.dot(xcat[rows(i, a), :], w1[pl.ds(a * 3 * width, 3 * width), :], preferred_element_type=F32)
         sigma = jax.nn.sigmoid(total)
-        slope[rows(i), :] = sigma * (1.0 + total * (1.0 - sigma))
         flipped = (total * sigma).astype(BF16).T
         for a in range(3):
             at[pl.ds(a * width, width), pl.ds(pl.multiple_of(i * size + (2 - a) * cols, cols), size)] = flipped
-
-    def backward(i, cat, weight):
-        total = jnp.zeros((size, width), F32)
-        for a in range(3):
-            for b in range(3):
-                total += lax.dot_general(
-                    cat[rows(i, a), b * width : (b + 1) * width],
-                    weight[pl.ds(((2 - a) * 3 + 2 - b) * width, width), :],
-                    (((1,), (1,)), ((), ())),
-                    preferred_element_type=F32,
-                )
-        return total
-
-    def kernel_grad(left, cat, first, count, full, half):
-        def one(b, carry):
-            value = jnp.dot(
-                left[...], cat[pl.ds(first, count), pl.ds(pl.multiple_of((2 - b) * width, width), width)], preferred_element_type=F32
-            )
-            for a in range(3):
-                for side in range(2):
-                    piece = value[a * width : (a + 1) * width, side * (width // 2) : (side + 1) * (width // 2)]
-                    where = pl.ds(pl.multiple_of((a * 3 + b) * width, width), width)
-                    full[side, where, :] = piece
-                    half[side, where, :] = piece.astype(BF16)
-            return carry
-
-        lax.fori_loop(0, 3, one, 0)
-
-    place = (dp, space, dp_count, space_count // 2)
-    first = Reduction(place, scale, (full1, half1, r11, h321, h161, r21, q321, q161, r31, out1), sems1)
-    second = Reduction(place, scale, (full2, half2, r12, h322, h162, r22, q322, q162, r32, out2), sems2)
-
-    blocks(forward)
-    kernel_grad(at, ccat, 0, (strip + 2) * cols, full2, half2)
-    second.start()
-
-    def hidden(i):
-        value = backward(i, ccat, w2) * slope[rows(i), :]
+        value = back[rows(i), :] * (sigma * (1.0 + total * (1.0 - sigma)))
         for j in range(block):
             put(hcat, pl.multiple_of(i * size + (j + 1) * cols, cols), value[j * cols : (j + 1) * cols], edge)
-
-    blocks(hidden)
-    edge_h[0] = hcat[pl.ds(strip * cols, cols), width : 2 * width]
-    edge_h[1] = hcat[pl.ds(cols, cols), width : 2 * width]
-    borders = [
-        make(edge_h.at[0], halo_h.at[0], halo_s.at[4], halo_r.at[4], device_id=down, device_id_type=MESH),
-        make(edge_h.at[1], halo_h.at[1], halo_s.at[5], halo_r.at[5], device_id=up, device_id_type=MESH),
-    ]
-    for copy in borders:
-        copy.start()
-    second.pair_to_dp()
-    kernel_grad(xt, hcat, cols, pixels, full1, half1)
-    first.start()
-    for copy in borders:
-        copy.wait_recv()
-    for side, p in ((0, 0), (1, strip + 1)):
-        put(hcat, p * cols, jnp.where(inside[side], halo_h[side].astype(F32), 0.0), edge)
-    first.pair_to_dp()
-    esum[...] = jnp.zeros_like(esum)
 
     def inputs(i):
         value = backward(i, hcat, w1)
@@ -373,8 +368,30 @@
         weighted = jnp.concatenate([lean] * (width // 128), axis=1) * value
         esum[...] += jnp.sum(weighted.reshape(size // 8, 8, width), axis=0)
 
-    blocks(inputs)
-    edp[dp] = esum[...]
+    loop(0, strip // block, forward)
+    edge_h[0] = hcat[pl.ds(strip * cols, cols), width : 2 * width]
+    edge_h[1] = hcat[pl.ds(cols, cols), width : 2 * width]
+    borders = sides_of(edge_h.at[0], edge_h.at[1], halo_h, 4)
+    start_sides(borders)
+
+    place = (dp, space, dp_count, space_count // 2)
+    depth = 3 // PIECES
+    pieces = []
+    for index in range(2 * PIECES):
+        of, b0 = divmod(index, PIECES)
+        base = b0 * depth * 3 * width
+        bufs = groups[index * 9 : index * 9 + 9]
+        pieces.append(Reduction(place, scale, base, (*bufs, (out2, out1)[of]), sems[index * 12 : index * 12 + 12]))
+
+    def grad_piece(index):
+        of, b0 = divmod(index, PIECES)
+        red = pieces[index]
+        for step in range(depth):
+            b = b0 * depth + step
+            left, cat, first, count = ((at, ccat, 0, (strip + 2) * cols), (xt, hcat, cols, pixels))[of]
+            kernel_grad(left, cat, first, count, b, red.full, red.half, step * 3 * width)
+        red.start()
+
     share_dp = Exchange(
         dp_count,
         lambda k, to: make(
@@ -382,13 +399,6 @@
             device_id=(lax.rem(dp + k, dp_count), space), device_id_type=MESH,
         ),
     )
-    share_dp.start()
-    second.dp_to_outer()
-    share_dp.wait_recv()
-    value = edp[0]
-    for k in range(1, dp_count):
-        value = value + edp[k]
-    esp[space] = value
     share_space = Exchange(
         space_count,
         lambda k, to: make(
@@ -396,24 +406,51 @@
             device_id=(dp, lax.rem(space + k, space_count)), device_id_type=MESH,
         ),
     )
-    share_space.start()
-    second.outer_to_gather()
-    first.dp_to_outer()
-    second.gather_dp()
-    first.outer_to_gather()
-    share_space.wait_recv()
-    value = lax.fori_loop(1, space_count, lambda k, v: v + esp[k], esp[0])
-    eout[...] = jnp.sum(value, axis=0, keepdims=True) * scale
-    first.gather_dp()
-    second.gather_pair()
-    first.gather_pair()
-    for copy in sides + borders:
-        copy.wait_send()
+
+    def borders_in():
+        wait_sides(borders)
+        for side, p in ((0, 0), (1, strip + 1)):
+            put(hcat, p * cols, jnp.where(inside[side], halo_h[side].astype(F32), 0.0), edge)
+        esum[...] = jnp.zeros_like(esum)
+
+    def embed_dp():
+        edp[dp] = esum[...]
+        share_dp.start()
+
+    def embed_space():
+        share_dp.wait_recv()
+        value = edp[0]
+        for k in range(1, dp_count):
+            value = value + edp[k]
+        esp[space] = value
+        share_space.start()
+
+    def embed_end():
+        share_space.wait_recv()
+        value = lax.fori_loop(1, space_count, lambda k, v: v + esp[k], esp[0])
+        eout[...] = jnp.sum(value, axis=0, keepdims=True) * scale
+
+    events = []
+    tick = 3 // PIECES
+    for index, red in enumerate(pieces):
+        at_tick = index * tick
+        events.append((at_tick, 1, functools.partial(grad_piece, index)))
+        ready = at_tick + tick
+        for delay, step in zip(DELAYS, (red.pair_to_dp, red.dp_to_outer, red.outer_to_gather, red.gather_dp, red.gather_pair)):
+            events.append((ready + delay, 0, step))
+    events.append((6, 2, borders_in))
+    for i in range(strip // block):
+        events.append((6 + i, 3, functools.partial(inputs, i)))
+    finished = 6 + strip // block
+    events += [(finished, 0, embed_dp), (finished + 4, 0, embed_space), (finished + 9, 0, embed_end)]
+    for _, _, step in sorted(events, key=lambda event: event[:2]):
+        step()
+    end_sides(sides + borders)
     peaks.wait_send()
     share_dp.wait_send()
     share_space.wait_send()
-    second.finish()
-    first.finish()
+    for red in pieces:
+        red.finish()
 
 
 def body(features, heights, cotangent, weight_first, weight_second, shade_embed):
@@ -426,14 +463,15 @@
     halo = (strip + 2) * cols
     taps = 9 * width
     lanes = width // 2
-    quarter = taps // dp_count
+    piece = taps // PIECES
+    quarter = piece // dp_count
     split = quarter % (16 * outer) == 0
     vmem = pltpu.VMEM
     dma = pltpu.SemaphoreType.DMA
     r3 = (outer - 1, quarter // outer, lanes) if split else (outer, quarter, lanes)
     reduction = [
-        vmem((2, taps, lanes), F32), vmem((2, taps, lanes), BF16), vmem((taps, lanes), BF16),
-        vmem((quarter, lanes), F32), vmem((taps, lanes), BF16), vmem((dp_count - 1, quarter, lanes), BF16),
+        vmem((2, piece, lanes), F32), vmem((2, piece, lanes), BF16), vmem((piece, lanes), BF16),
+        vmem((quarter, lanes), F32), vmem((piece, lanes), BF16), vmem((dp_count - 1, quarter, lanes), BF16),
         vmem((quarter, lanes), F32), vmem((quarter, lanes), BF16), vmem(r3, BF16),
     ]
     pairs = [1, dp_count - 1, outer - 1, outer - 1, dp_count - 1, 1]
@@ -444,19 +482,19 @@
         vmem((128, cols), F32), vmem((pixels, 128), F32),
         vmem((halo, 3 * width), BF16), vmem((halo, 3 * width), BF16), vmem((halo, 3 * width), BF16),
         vmem((3 * width, pixels), BF16), vmem((3 * width, halo), BF16), vmem((pixels, width), F32),
-        *reduction, *reduction,
         vmem((8, width), F32), vmem((dp_count, 8, width), F32), vmem((space_count, 8, width), F32),
         dma((6,)), dma((6,)), dma((space_count - 1,)), dma((space_count - 1,)),
         dma((dp_count - 1,)), dma((dp_count - 1,)), dma((space_count - 1,)), dma((space_count - 1,)),
-        *phase_sems, *phase_sems,
+        *(reduction * (2 * PIECES)),
+        *(phase_sems * (2 * PIECES)),
     ]
     spec = pl.BlockSpec(memory_space=pltpu.VMEM)
     gfeat, first, second, total = pl.pallas_call(
         functools.partial(kernel, (dp_count, space_count), scale, 2.0 / total_rows),
         out_shape=(
             jax.ShapeDtypeStruct((pixels, width), BF16),
-            jax.ShapeDtypeStruct((2, taps, lanes), BF16),
-            jax.ShapeDtypeStruct((2, taps, lanes), BF16),
+            jax.ShapeDtypeStruct((taps, width), BF16),
+            jax.ShapeDtypeStruct((taps, width), BF16),
             jax.ShapeDtypeStruct((1, width), F32),
         ),
         in_specs=[spec] * 6,
@@ -470,11 +508,11 @@
         cotangent.reshape(pixels, width),
         weight_first.reshape(taps, width),
         weight_second.reshape(taps, width),
-        shade_embed.reshape(1, width),
+        shade_embed,
     )
 
-    def joined(halves):
-        return jnp.concatenate([halves[0], halves[1]], axis=1).astype(F32).reshape(3, 3, width, width)
+    def joined(pieces):
+        return jnp.swapaxes(pieces.reshape(3, 3, width, width), 0, 1).astype(F32)
 
     return gfeat.reshape(features.shape), joined(first), joined(second), total.reshape(width)
 

time: 73.4 us -> 62.6 us (0.85)
  Pallas kernels: 64.9 us -> 55.8 us
  local copies, waits for them, and re-layouts: 4.52 us -> 1.54 us
  other arithmetic: 3.14 us -> 4.43 us
    pallas_call x1, Pallas kernels: 64.9 us -> 55.8 us  [body(): pl.pallas_call(functools.partial(kernel, (dp_count, space_count), scale,...]
    slice x1 -> x0, local copies, waits for them, and re-layouts: 1.75 us -> none  [joined(): halves[0]]
    convert_element_type x2 -> x1, other arithmetic: 3.14 us -> 4.43 us  [joined(): return jnp.swapaxes(pieces.reshape(3, 3, width, width), 0, 1).astype(F32)]
    reshape x1 -> x0, local copies, waits for them, and re-layouts: 1.22 us -> none  [body(): shade_embed.reshape(1, width)]
where the time goes in v2:
time: 62.6 us; the launch traced here: 62.4 us
  Pallas kernels  55.8 us (89%)
  other arithmetic  4.43 us (7%)
  local copies, waits for them, and re-layouts  1.54 us (2%)
  between operations  0.66 us (1%)
    pallas_call x1, Pallas kernels, body(): pl.pallas_call(functools.partial(kernel, (dp_count, space_count), scale,...  55.8 us
    convert_element_type x1, other arithmetic, joined(): return jnp.swapaxes(pieces.reshape(3, 3, width, width), 0, 1).astype(F32)  4.43 us
    unnamed x6, local copies, waits for them, and re-layouts  1.54 us

profile of v2, /device:TPU:0, one launch (start us, length us, event | category | flops | bytes accessed | tf_op | source)
XLA Modules:
  0.0 62.4 jit_solution(17960227226330001036)
XLA Ops:
  0.6 55.8 %shard_map.93 = (bf16[2048,256]{1,0:T(8,128)(2,1)}, bf16[2304,256]{1,0:T(8,128)(2,1)}, bf16[2304,256]{1,0:T(8,128)(2,1)}, f32[1,256]{1,0:T(1,128)}) custom-call(bf16[2048,256]{1,0:T(8,128)(2,1)} %bitcast.21, f32[16,128]{1,0:T(8,128)} %bitcast.23, bf16[2048,256]{1,0:T(8,128)(2,1)} %bitcast.22, bf16[2304,256]{1,0:T(8,128)(2,1)} %bitcast.19, ...), custom_call_target="tpu_custom_call" | custom-call | flops 12079595520 | bytes 16777216 | tf_op jit(solution)/shard_map/pallas_call | solution.py:492
  56.4 0.0 copy-start
  56.4 0.0 copy-start.1
  56.4 4.4 %copy_bitcast_fusion = (f32[3,3,256,256]{3,2,1,0:T(8,128)}, f32[3,3,256,256]{3,2,1,0:T(8,128)}) fusion(bf16[3,3,256,256]{3,2,1,0:T(8,128)(2,1)} %bitcast.15, bf16[3,3,256,256]{3,2,1,0:T(8,128)(2,1)} %bitcast.16), kind=kLoop, calls=%fused_computation | loop fusion | flops 1179648 | bytes 7077888 | tf_op jit(solution)/shard_map/convert_element_type | solution.py:515
  60.9 0.0 copy-done
  60.9 1.0 %copy.16 = bf16[1,16,128,256]{3,2,1,0:T(8,128)(2,1)} copy(bf16[1,16,128,256]{3,2,1,0:T(8,128)(2,1)S(1)} %bitcast.17) | data formatting | bytes 2097152
  61.8 0.0 copy-done.1
  61.8 0.6 copy.17
Async XLA Ops:
  56.4 4.4 %copy-start = (bf16[2048,256]{1,0:T(8,128)(2,1)S(1)}, bf16[2048,256]{1,0:T(8,128)(2,1)}, u32[]{:S(2)}) copy-start(bf16[2048,256]{1,0:T(8,128)(2,1)} %get-tuple-element.8) | copy-start | bytes 3145732
  56.4 5.4 %copy-start.1 = (f32[1,256]{1,0:T(1,128)S(1)}, f32[1,256]{1,0:T(1,128)}, u32[]{:S(2)}) copy-start(f32[1,256]{1,0:T(1,128)} %get-tuple-element.11) | copy-start | bytes 3076

commit v3 on v2

--- a/solution.py
+++ b/solution.py
@@ -49,7 +49,7 @@
         self.full, self.half, self.r1, self.h32, self.h16, self.r2, self.q32, self.q16, self.r3, self.out = bufs
         self.base = base
         self.scale = scale
-        rows, lanes = self.full.shape[1:]
+        rows, lanes = self.full.shape[2:]
         mine = pl.ds(pl.multiple_of(self.core * lanes, lanes), lanes)
         theirs = pl.ds(pl.multiple_of((1 - self.core) * lanes, lanes), lanes)
         self.mine = mine
@@ -60,8 +60,8 @@
         core, dp, outer, quarter = self.core, self.dp, self.outer, self.quarter
         sibling = (dp, outer * 2 + 1 - core)
 
-        def rows_of(index, size, start=0):
-            return pl.ds(pl.multiple_of(start + index * size, 16), size)
+        def rows_of(index, size):
+            return pl.ds(pl.multiple_of(index * size, 16), size)
 
         self.rows_of = rows_of
         make = pltpu.make_async_remote_copy
@@ -79,28 +79,28 @@
             return (dp, outer_at(k, True) * 2 + core)
 
         def spot(o):
-            start = base + dp * quarter + (o * self.part if self.split else 0)
+            start = dp * quarter + (o * self.part if self.split else 0)
             return pl.ds(pl.multiple_of(start, 16), self.part)
 
         self.spot = spot
         self.dp_at = dp_at
         self.s1 = Exchange(2, lambda k, to: make(self.half.at[1 - core], self.r1, pair_s.at[0], pair_r.at[0], device_id=sibling, device_id_type=MESH))
         self.s2_make = lambda k, to: make(
-            self.h16.at[rows_of(dp_at(k, True), quarter)], self.r2.at[k - 1], dp_s.at[k - 1], dp_r.at[k - 1], device_id=dp_id(k), device_id_type=MESH
+            self.h16.at[:, rows_of(dp_at(k, True), quarter)], self.r2.at[k - 1], dp_s.at[k - 1], dp_r.at[k - 1], device_id=dp_id(k), device_id_type=MESH
         )
         self.s2 = Exchange(self.dp_count, self.s2_make)
         if self.split:
             self.s3 = Exchange(
                 self.outer_count,
                 lambda k, to: make(
-                    self.q16.at[rows_of(outer_at(k, True), self.part)], self.r3.at[k - 1], out_s.at[k - 1], out_r.at[k - 1], device_id=outer_id(k), device_id_type=MESH
+                    self.q16.at[:, rows_of(outer_at(k, True), self.part)], self.r3.at[k - 1], out_s.at[k - 1], out_r.at[k - 1], device_id=outer_id(k), device_id_type=MESH
                 ),
             )
             self.g3 = Exchange(
                 self.outer_count,
                 lambda k, to: make(
-                    self.out.at[spot(outer), mine],
-                    self.out.at[spot(outer if to else outer_at(k, False)), mine],
+                    self.out.at[:, base, spot(outer), mine],
+                    self.out.at[:, base, spot(outer if to else outer_at(k, False)), mine],
                     gout_s.at[k - 1], gout_r.at[k - 1], device_id=outer_id(k), device_id_type=MESH,
                 ),
             )
@@ -115,15 +115,15 @@
         self.g2 = Exchange(
             self.dp_count,
             lambda k, to: make(
-                self.out.at[rows_of(dp, quarter, base), mine],
-                self.out.at[rows_of(dp if to else dp_at(k, False), quarter, base), mine],
+                self.out.at[:, base, rows_of(dp, quarter), mine],
+                self.out.at[:, base, rows_of(dp if to else dp_at(k, False), quarter), mine],
                 gdp_s.at[k - 1], gdp_r.at[k - 1], device_id=dp_id(k), device_id_type=MESH,
             ),
         )
         self.g1 = Exchange(
             2,
             lambda k, to: make(
-                self.out.at[pl.ds(base, rows), mine], self.out.at[pl.ds(base, rows), mine if to else theirs], gpair_s.at[0], gpair_r.at[0], device_id=sibling, device_id_type=MESH
+                self.out.at[:, base, :, mine], self.out.at[:, base, :, mine if to else theirs], gpair_s.at[0], gpair_r.at[0], device_id=sibling, device_id_type=MESH
             ),
         )
 
@@ -135,12 +135,12 @@
 
         def total(index):
             where = self.rows_of(index, self.quarter)
-            value = self.full[self.core, where, :] + self.r1[where, :].astype(F32)
+            value = self.full[self.core, :, where, :] + self.r1[:, where, :].astype(F32)
             return where, value
 
         for k in range(1, self.dp_count):
             where, value = total(self.dp_at(k, True))
-            self.h16[where, :] = value.astype(BF16)
+            self.h16[:, where, :] = value.astype(BF16)
             self.s2_make(k, True).start()
         _, value = total(self.dp)
         self.h32[...] = value
@@ -157,15 +157,15 @@
     def outer_to_gather(self):
         self.s3.wait_recv()
         if self.split:
-            value = self.q32[self.rows_of(self.outer, self.part), :]
+            value = self.q32[:, self.rows_of(self.outer, self.part), :]
             for k in range(1, self.outer_count):
                 value = value + self.r3[k - 1].astype(F32)
-            self.out[self.spot(self.outer), self.mine] = (value * self.scale).astype(BF16)
+            self.out[:, self.base, self.spot(self.outer), self.mine] = (value * self.scale).astype(BF16)
             self.g3.start()
         else:
             self.r3[self.outer] = self.q16[...]
             value = lax.fori_loop(0, self.outer_count, lambda j, v: v + self.r3[j].astype(F32), jnp.zeros(self.q32.shape, F32))
-            self.out[self.spot(self.outer), self.mine] = (value * self.scale).astype(BF16)
+            self.out[:, self.base, self.spot(self.outer), self.mine] = (value * self.scale).astype(BF16)
 
     def gather_dp(self):
         if self.g3 is not None:
@@ -191,14 +191,18 @@
     cat[rows, 2 * width :] = jnp.where(edge == count - 1, 0.0, pltpu.roll(value, count - 1, 0)).astype(BF16)
 
 
-def kernel(counts, scale, decline, feat, high, cot, w1, w2, embed, gfeat, out1, out2, eout, *scratch):
+def kernel(counts, scale, decline, feat, high, cot, w1_in, w2_in, embed, gfeat, out1, out2, eout, *scratch):
     dp_count, space_count = counts
     (
         stat, stats, halo_f, halo_c, halo_h, edge_h, shade, wide_shade, xcat, ccat, hcat, xt, at, back,
         esum, edp, esp,
-        halo_s, halo_r, stat_s, stat_r, edp_s, edp_r, esp_s, esp_r,
-    ) = scratch[:25]
-    groups, sems = scratch[25 : 25 + 18 * PIECES], scratch[25 + 18 * PIECES :]
+        halo_s, halo_r, stat_s, stat_r, edp_s, edp_r, esp_s, esp_r, w1, w2, w_s,
+    ) = scratch[:28]
+    groups, sems = scratch[28 : 28 + 18 * PIECES], scratch[28 + 18 * PIECES :]
+    load1 = pltpu.make_async_copy(w1_in, w1, w_s.at[0])
+    load2 = pltpu.make_async_copy(w2_in, w2, w_s.at[1])
+    load2.start()
+    load1.start()
     dp, space = lax.axis_index("dp"), lax.axis_index("space")
     strip, cols = high.shape
     width = feat.shape[1]
@@ -299,6 +303,7 @@
     def back_act(i):
         back[rows(i), :] = backward(i, ccat, w2)
 
+    load2.wait()
     loop(1, strip // block - 1, back_act)
 
     peaks.wait_recv()
@@ -342,12 +347,12 @@
             if 0 <= p - offset < strip:
                 xt[pl.ds(offset * width, width), pl.ds((p - offset) * cols, cols)] = flipped
 
-    def kernel_grad(left, cat, first, count, b, full, half, row):
+    def kernel_grad(left, cat, first, count, b, full, half):
         value = jnp.dot(left[...], cat[pl.ds(first, count), (2 - b) * width : (3 - b) * width], preferred_element_type=F32)
         for side in range(2):
-            piece = value[:, side * (width // 2) : (side + 1) * (width // 2)]
-            full[side, pl.ds(row, 3 * width), :] = piece
-            half[side, pl.ds(row, 3 * width), :] = piece.astype(BF16)
+            piece = value[:, side * (width // 2) : (side + 1) * (width // 2)].reshape(3, width, width // 2)
+            full[side] = piece
+            half[side] = piece.astype(BF16)
 
     def forward(i):
         total = jnp.zeros((size, width), F32)
@@ -368,6 +373,7 @@
         weighted = jnp.concatenate([lean] * (width // 128), axis=1) * value
         esum[...] += jnp.sum(weighted.reshape(size // 8, 8, width), axis=0)
 
+    load1.wait()
     loop(0, strip // block, forward)
     edge_h[0] = hcat[pl.ds(strip * cols, cols), width : 2 * width]
     edge_h[1] = hcat[pl.ds(cols, cols), width : 2 * width]
@@ -376,12 +382,12 @@
 
     place = (dp, space, dp_count, space_count // 2)
     depth = 3 // PIECES
+    assert depth == 1
     pieces = []
     for index in range(2 * PIECES):
         of, b0 = divmod(index, PIECES)
-        base = b0 * depth * 3 * width
         bufs = groups[index * 9 : index * 9 + 9]
-        pieces.append(Reduction(place, scale, base, (*bufs, (out2, out1)[of]), sems[index * 12 : index * 12 + 12]))
+        pieces.append(Reduction(place, scale, b0, (*bufs, (out2, out1)[of]), sems[index * 12 : index * 12 + 12]))
 
     def grad_piece(index):
         of, b0 = divmod(index, PIECES)
@@ -389,7 +395,7 @@
         for step in range(depth):
             b = b0 * depth + step
             left, cat, first, count = ((at, ccat, 0, (strip + 2) * cols), (xt, hcat, cols, pixels))[of]
-            kernel_grad(left, cat, first, count, b, red.full, red.half, step * 3 * width)
+            kernel_grad(left, cat, first, count, b, red.full, red.half)
         red.start()
 
     share_dp = Exchange(
@@ -463,16 +469,15 @@
     halo = (strip + 2) * cols
     taps = 9 * width
     lanes = width // 2
-    piece = taps // PIECES
-    quarter = piece // dp_count
+    quarter = width // dp_count
     split = quarter % (16 * outer) == 0
     vmem = pltpu.VMEM
     dma = pltpu.SemaphoreType.DMA
-    r3 = (outer - 1, quarter // outer, lanes) if split else (outer, quarter, lanes)
+    r3 = (outer - 1, 3, quarter // outer, lanes) if split else (outer, 3, quarter, lanes)
     reduction = [
-        vmem((2, piece, lanes), F32), vmem((2, piece, lanes), BF16), vmem((piece, lanes), BF16),
-        vmem((quarter, lanes), F32), vmem((piece, lanes), BF16), vmem((dp_count - 1, quarter, lanes), BF16),
-        vmem((quarter, lanes), F32), vmem((quarter, lanes), BF16), vmem(r3, BF16),
+        vmem((2, 3, width, lanes), F32), vmem((2, 3, width, lanes), BF16), vmem((3, width, lanes), BF16),
+        vmem((3, quarter, lanes), F32), vmem((3, width, lanes), BF16), vmem((dp_count - 1, 3, quarter, lanes), BF16),
+        vmem((3, quarter, lanes), F32), vmem((3, quarter, lanes), BF16), vmem(r3, BF16),
     ]
     pairs = [1, dp_count - 1, outer - 1, outer - 1, dp_count - 1, 1]
     phase_sems = [dma((count,)) for count in pairs for _ in range(2)]
@@ -485,6 +490,7 @@
         vmem((8, width), F32), vmem((dp_count, 8, width), F32), vmem((space_count, 8, width), F32),
         dma((6,)), dma((6,)), dma((space_count - 1,)), dma((space_count - 1,)),
         dma((dp_count - 1,)), dma((dp_count - 1,)), dma((space_count - 1,)), dma((space_count - 1,)),
+        vmem((taps, width), BF16), vmem((taps, width), BF16), dma((2,)),
         *(reduction * (2 * PIECES)),
         *(phase_sems * (2 * PIECES)),
     ]
@@ -493,11 +499,11 @@
         functools.partial(kernel, (dp_count, space_count), scale, 2.0 / total_rows),
         out_shape=(
             jax.ShapeDtypeStruct((pixels, width), BF16),
-            jax.ShapeDtypeStruct((taps, width), BF16),
-            jax.ShapeDtypeStruct((taps, width), BF16),
+            jax.ShapeDtypeStruct((3, 3, width, width), BF16),
+            jax.ShapeDtypeStruct((3, 3, width, width), BF16),
             jax.ShapeDtypeStruct((1, width), F32),
         ),
-        in_specs=[spec] * 6,
+        in_specs=[spec] * 3 + [pl.BlockSpec(memory_space=pl.ANY)] * 2 + [spec],
         out_specs=(spec,) * 4,
         scratch_shapes=scratch,
         compiler_params=pltpu.CompilerParams(collective_id=0, has_side_effects=True, vmem_limit_bytes=60 * 2**20),
@@ -511,10 +517,7 @@
         shade_embed,
     )
 
-    def joined(pieces):
-        return jnp.swapaxes(pieces.reshape(3, 3, width, width), 0, 1).astype(F32)
-
-    return gfeat.reshape(features.shape), joined(first), joined(second), total.reshape(width)
+    return gfeat.reshape(features.shape), first.astype(F32), second.astype(F32), total.reshape(width)
 
 
 def solution(mesh):

time: 62.6 us -> 62.1 us (level)
  Pallas kernels: 55.8 us -> 55.1 us
    pallas_call x1, Pallas kernels: 55.8 us -> 55.1 us  [body(): pl.pallas_call(functools.partial(kernel, (dp_count, space_count), scale,...]
    convert_element_type x1 -> x2, other arithmetic: 4.43 us -> 4.62 us  [the longest x1 2.99 us: body(): first.astype(F32)]
    unnamed x6 -> x8, local copies, waits for them, and re-layouts: 1.54 us -> 1.54 us
where the time goes in v3:
time: 62.1 us; the launch traced here: 61.9 us
  Pallas kernels  55.1 us (89%)
  other arithmetic  4.62 us (7%)
  local copies, waits for them, and re-layouts  1.54 us (2%)
  between operations  0.65 us (1%)
    pallas_call x1, Pallas kernels, body(): pl.pallas_call(functools.partial(kernel, (dp_count, space_count), scale,...  55.1 us
    convert_element_type x1, other arithmetic, body(): first.astype(F32)  2.99 us
    convert_element_type x1, other arithmetic, body(): second.astype(F32)  1.63 us
    unnamed x8, local copies, waits for them, and re-layouts  1.54 us

profile of v3, /device:TPU:0, one launch (start us, length us, event | category | flops | bytes accessed | tf_op | source)
XLA Modules:
  0.0 61.9 jit_solution(9210955221961492261)
XLA Ops:
  0.6 55.1 %shard_map.93 = (bf16[2048,256]{1,0:T(8,128)(2,1)}, bf16[3,3,256,256]{3,2,1,0:T(8,128)(2,1)}, bf16[3,3,256,256]{3,2,1,0:T(8,128)(2,1)}, f32[1,256]{1,0:T(1,128)}) custom-call(bf16[2048,256]{1,0:T(8,128)(2,1)} %bitcast.11, f32[16,128]{1,0:T(8,128)} %bitcast.13, bf16[2048,256]{1,0:T(8,128)(2,1)} %bitcast.12, bf16[2304,256]{1,0:T(8,128)(2,1)} %bitcast.9, ...), custom_call_target="tpu_custom_call" | custom-call | flops 12079595520 | bytes 16777216 | tf_op jit(solution)/shard_map/pallas_call | solution.py:498
  55.7 0.0 copy-start
  55.7 3.0 %convert_element_type.6 = f32[3,3,256,256]{3,2,1,0:T(8,128)} convert(bf16[3,3,256,256]{3,2,1,0:T(8,128)(2,1)} %get-tuple-element.9) | non-fusion elementwise | flops 589824 | bytes 3538944 | tf_op jit(solution)/shard_map/convert_element_type | solution.py:520
  58.7 0.0 copy-done
  58.7 0.0 copy-start.1
  58.7 1.6 %convert_element_type.7 = f32[3,3,256,256]{3,2,1,0:T(8,128)} convert(bf16[3,3,256,256]{3,2,1,0:T(8,128)(2,1)S(1)} %copy-done) | non-fusion elementwise | flops 589824 | bytes 3538944 | tf_op jit(solution)/shard_map/convert_element_type | solution.py:520
  60.4 0.0 copy-done.1
  60.4 0.0 copy-start.2
  60.4 1.0 %copy.12 = bf16[1,16,128,256]{3,2,1,0:T(8,128)(2,1)} copy(bf16[1,16,128,256]{3,2,1,0:T(8,128)(2,1)S(1)} %bitcast.7) | data formatting | bytes 2097152
  61.3 0.0 copy-done.2
  61.3 0.6 copy.13
Async XLA Ops:
  55.7 3.0 %copy-start = (bf16[3,3,256,256]{3,2,1,0:T(8,128)(2,1)S(1)}, bf16[3,3,256,256]{3,2,1,0:T(8,128)(2,1)}, u32[]{:S(2)}) copy-start(bf16[3,3,256,256]{3,2,1,0:T(8,128)(2,1)} %get-tuple-element.10) | copy-start | bytes 3538948
  58.7 1.6 %copy-start.1 = (bf16[2048,256]{1,0:T(8,128)(2,1)S(1)}, bf16[2048,256]{1,0:T(8,128)(2,1)}, u32[]{:S(2)}) copy-start(bf16[2048,256]{1,0:T(8,128)(2,1)} %get-tuple-element.8) | copy-start | bytes 3145732
  60.4 1.0 %copy-start.2 = (f32[1,256]{1,0:T(1,128)S(1)}, f32[1,256]{1,0:T(1,128)}, u32[]{:S(2)}) copy-start(f32[1,256]{1,0:T(1,128)} %get-tuple-element.11) | copy-start | bytes 3076
